TPU v7x, 32 devices: a whole 2x2x4 slice. The times are simulated.
32 devices in a mesh: parts: 2 (over y), nest: 4 (over z), tx: 4 (over x, core).
Axes of the slice: x: 2, y: 2, z: 4, core: 2. Of those that a mesh axis runs over, the one named last changes fastest.
Arguments:
- model_state: float32 [96, 256, 512], P('parts', 'nest', 'tx'), parts along dimension 0, may hold values from -6 to 6
- diffusivity: float32 [512, 512], P(('parts', 'nest'), 'tx'), parts along dimension 0, may hold values from 0.05 to 0.24
- rim_index: int32 [16, 512], P('nest', 'tx'), may hold values from 0 to 4095
- rim_weight: float32 [16, 512], P('nest', 'tx'), may hold values from 0.05 to 0.5
- side_index: int32 [16, 128], P('nest'), may hold values from 0 to 4095
- side_weight: float32 [16, 128], P('nest'), may hold values from 0.05 to 0.5
- rim_tile: int32 [4, 4], P('nest', 'tx'), may hold values from 0 to 1
- nest_offset: int32 [2], replicated, may hold values from 0 to 4095
Outputs:
- new_state: float32 [96, 256, 512], P('parts', 'nest', 'tx'), parts along dimension 0
There are 2 independent parts, one for each index of `parts`. A program takes and returns all parts, laid end to end along the dimension named above; an argument that names none is the same for every part. Nothing has to cross between parts.
Inputs may be any that keep to these rules, and one draw needn't show every extreme that they name: Sources are counted from their grid's offset: rim_index plus nest_offset of its grid stays below 8192. Sources are counted from their grid's offset: side_index plus nest_offset of its grid stays below 8192. `nest_offset`: the parent's entry is not read.
All inputs are finite; a program needn't handle non-finite values.
Results may differ from a plain program's by a relative error of at most 0.0001.
Values sent between devices are 32-bit elements; how exact they have to be, the bound alone decides.
A program may use at most 128 MiB of HBM per device.

v0:
```python
import jax
import jax.numpy as jnp
from jax import lax
from jax.sharding import PartitionSpec as P

STEPS = 2


def broadcast(block, axis, holder):
    block = jnp.where(lax.axis_index(axis) == holder, block, jnp.zeros_like(block))
    return lax.psum(block, axis)


def partner(value, axis, stride):
    mask = 2**stride
    pairs = [(source, source ^ mask) for source in range(lax.axis_size(axis))]
    return lax.ppermute(value, axis, pairs)


def padded_2(cells, sides, width):
    for axis, dim in sides:
        count = lax.axis_size(axis)
        head = lax.slice_in_dim(cells, 0, width, axis=dim)
        tail = lax.slice_in_dim(cells, cells.shape[dim] - width, cells.shape[dim], axis=dim)
        cells = jnp.concatenate(
            [
                lax.ppermute(tail, axis, [(i, (i + 1) % count) for i in range(count)]),
                cells,
                lax.ppermute(head, axis, [((i + 1) % count, i) for i in range(count)]),
            ],
            axis=dim,
        )
    return cells


def interpolate(flat_tile, flat_index, weights):
    picked = jnp.take(flat_tile, flat_index.reshape(-1), axis=1)
    picked = picked.reshape((flat_tile.shape[0],) + flat_index.shape)
    return jnp.sum(picked * weights[None], axis=-2)


def per_device(
    model_state, diffusivity, rim_index, rim_weight, side_index, side_weight, rim_tile, nest_offset
):
    fields = model_state
    var_count, tile_rows, tile_cols = fields.shape
    my_index = lax.axis_index("nest")
    column_index = lax.axis_index("tx")
    column_count = lax.axis_size("tx")
    parity = my_index % 2
    is_parent = my_index < 2
    group_ids = jnp.arange(nest_offset.shape[0])
    my_offset = jnp.sum(jnp.where(group_ids == my_index // 2, nest_offset, 0))
    for step_index in range(STEPS):
        parent_tiles = [broadcast(fields, "nest", root_row) for root_row in range(2)]
        chosen = jnp.where(rim_tile[0, 0] == 1, parent_tiles[1], parent_tiles[0]).reshape(
            var_count, tile_rows * tile_cols
        )
        rim_values = interpolate(chosen, rim_index + my_offset, rim_weight)
        side_values = interpolate(chosen, side_index + my_offset, side_weight)
        outward = jnp.where(parity == 0, fields[:, -1], fields[:, 0])
        partner_row = partner(outward, "nest", 0)
        outer_top = jnp.where(is_parent, fields[:, 0], rim_values)
        outer_bottom = jnp.where(is_parent, fields[:, -1], rim_values)
        top_ghost = jnp.where(parity == 0, outer_top, partner_row)
        bottom_ghost = jnp.where(parity == 0, partner_row, outer_bottom)
        padded = padded_2(fields, (("tx", 2),), 1)
        use_left = jnp.logical_not(is_parent) & (column_index == 0)
        use_right = jnp.logical_not(is_parent) & (column_index == column_count - 1)
        left_ghost = jnp.where(use_left, side_values[:, :tile_rows], padded[:, :, 0])
        right_ghost = jnp.where(use_right, side_values[:, tile_rows:], padded[:, :, -1])
        left_side = jnp.concatenate([left_ghost[:, :, None], fields[:, :, :-1]], axis=2)
        right_side = jnp.concatenate([fields[:, :, 1:], right_ghost[:, :, None]], axis=2)
        above = jnp.concatenate([top_ghost[:, None], fields[:, :-1]], axis=1)
        below_rows = jnp.concatenate([fields[:, 1:], bottom_ghost[:, None]], axis=1)
        laplace = above + below_rows + left_side + right_side - 4.0 * fields
        fields = fields + diffusivity[None] * laplace
    return fields


def solution(mesh):
    placed = (
        P("parts", "nest", "tx"),
        P(("parts", "nest"), "tx"),
        P("nest", "tx"),
        P("nest", "tx"),
        P("nest", None),
        P("nest", None),
        P("nest", "tx"),
        P(),
    )
    return jax.shard_map(
        per_device, mesh=mesh, in_specs=placed, out_specs=P("parts", "nest", "tx"), check_vma=False
    )
```

profile of v0, /device:TPU:16, one launch (start us, length us, event | category | flops | bytes accessed | tf_op | source)
XLA Modules:
  0.0 663.2 jit_solution(15282430780521904792)
XLA Ops:
  6.5 0.0 all-reduce.7.cloned.1.call-start
  6.5 3.7 copy.264
  10.3 6.8 %broadcast_select_fusion.2 = (f32[48,64,128]{0,2,1:T(8,128)}, f32[48,64,128]{0,2,1:T(8,128)}) fusion(f32[48,64,128]{0,2,1:T(8,128)} %copy.264, pred[]{:T(512)S(6)} %eq.43, pred[]{:T(512)S(6)} %eq.42), kind=kLoop, calls=%fused_computation.18 | loop fusion | flops 786432 | bytes 4718594 | tf_op jit(solution)/shard_map/jit(_where)/select_n | solution.py:10
  17.1 0.0 all-reduce.7.cloned.1.call-update
  17.1 0.0 all-reduce.5.cloned.1.call-start
  17.2 1.0 fusion.10
  18.2 0.0 copy-start.9
  18.2 0.0 copy-start.7
  18.2 0.0 copy-start.8
  18.2 1.6 collective-permute-start
  19.8 0.0 copy-done.3
  19.9 1.7 fusion.19
  21.6 2.2 copy.283
  23.8 0.0 collective-permute-start.1
  23.8 0.9 copy.284
  24.7 1.8 collective-permute-start.2
  27.1 0.0 copy-done.9
  27.1 0.6 fusion.12
  27.8 0.0 copy-done.7
  27.8 0.0 copy-done.8
  27.8 0.6 compare_and_fusion
  28.4 0.0 copy-start.2
  28.4 8.0 %fusion.17 = (f32[48,63,128]{0,2,1:T(8,128)}, f32[48,63,128]{0,2,1:T(8,128)}) fusion(f32[48,64,128]{0,2,1:T(8,128)} %copy.264), kind=kLoop, calls=%fused_computation.55 | loop fusion | bytes 6193152 | tf_op jit(solution)/shard_map/slice | solution.py:74
  36.4 4.2 fusion.18
  40.6 268.3 %all-reduce.7.cloned.1.call-done = (f32[48,64,128]{0,2,1:T(8,128)}, f32[48,64,128]{0,2,1:T(8,128)}) async-done(((f32[48,64,128]{0,2,1:T(8,128)}, f32[48,64,128]{0,2,1:T(8,128)}), (f32[48,64,128]{0,2,1:T(8,128)}, f32[48,64,128]{0,2,1:T(8,128)})) %all-reduce.7.cloned.1.call-update) | async-done | bytes 3145744 | tf_op jit(solution)/shard_map/psum | solution.py:11
  308.9 5.3 broadcast_select_fusion.5
  314.2 3.2 gather_fusion
  317.4 3.2 gather_fusion.1
  320.7 0.1 broadcast_select_fusion.9
  320.8 0.1 broadcast_select_fusion.8
  321.0 0.1 multiply_reduce_fusion.3
  321.1 0.0 collective-permute-done
  321.1 0.9 select_bitcast_fusion.3
  322.0 0.1 multiply_reduce_fusion.2
  322.2 0.0 collective-permute-done.1
  322.2 0.0 collective-permute-done.2
  322.2 11.0 %broadcast_select_fusion = (f32[48,64,128]{0,2,1:T(8,128)}, f32[48,64,128]{0,2,1:T(8,128)S(1)}) fusion(pred[]{:T(512)S(6)} %eq.43, f32[48,64,128]{0,2,1:T(8,128)} %copy.264, f32[48,64,1]{0,2,1:T(1,128)S(1)} %bitcast.82, f32[48,64,127]{0,2,1:T(8,128)} %get-tuple-element.29, f32[48,64,127]{0,2,1:T(8,128)} %get-tuple-element.28, f32[48,64,1]{0,2,1:T(1,128)S(1)} %bitcast.81, ...), kind=kLoop, calls=%fused_computation.16 | loop fusion | flops 4718592 | bytes 11042817 | tf_op jit(solution)/shard_map/jit(_where)/select_n | solution.py:10
  333.2 2.8 broadcast_select_fusion.1
  336.0 0.4 copy-done
  336.4 0.0 all-reduce.5.cloned.1.call-update
  336.5 1.1 fusion.15
  337.6 0.1 copy.265
  337.6 0.0 collective-permute-start.4
  337.6 0.1 copy.269
  337.7 1.9 collective-permute-start.5
  339.7 8.5 %fusion.16 = (f32[48,63,128]{0,2,1:T(8,128)}, f32[48,63,128]{0,2,1:T(8,128)}) fusion(f32[48,64,128]{0,2,1:T(8,128)} %copy-done), kind=kLoop, calls=%fused_computation.54 | loop fusion | bytes 6193152 | tf_op jit(solution)/shard_map/slice | solution.py:75
  348.1 4.1 fusion.14
  352.3 0.1 collective-permute-start.3
  352.4 0.0 collective-permute-done.4
  352.4 0.1 copy.266
  352.4 0.0 collective-permute-done.5
  352.5 0.1 copy.270
  352.5 276.0 %all-reduce.5.cloned.1.call-done = (f32[48,64,128]{0,2,1:T(8,128)}, f32[48,64,128]{0,2,1:T(8,128)}) async-done(((f32[48,64,128]{0,2,1:T(8,128)}, f32[48,64,128]{0,2,1:T(8,128)}), (f32[48,64,128]{0,2,1:T(8,128)}, f32[48,64,128]{0,2,1:T(8,128)})) %all-reduce.5.cloned.1.call-update) | async-done | bytes 3145744 | tf_op jit(solution)/shard_map/psum | solution.py:11
  628.5 5.2 broadcast_select_fusion.4
  633.8 3.2 gather_fusion.3
  637.0 3.2 gather_fusion.2
  640.2 0.1 broadcast_select_fusion.6
  640.4 0.1 multiply_reduce_fusion
  640.5 0.1 broadcast_select_fusion.7
  640.7 0.1 multiply_reduce_fusion.1
  640.8 0.0 collective-permute-done.3
  640.8 0.9 select_bitcast_fusion
  641.7 10.7 %fusion.9 = f32[48,64,128]{0,2,1:T(8,128)} fusion(f32[48,64,128]{0,2,1:T(8,128)} %copy-done, f32[48,63,128]{0,2,1:T(8,128)} %get-tuple-element.25, f32[48,1,128]{0,2,1:T(8,128)S(1)} %get-tuple-element.17, f32[48,1,128]{0,2,1:T(8,128)S(1)} %get-tuple-element.16, f32[48,63,128]{0,2,1:T(8,128)} %get-tuple-element.24, f32[48,64,127]{0,2,1:T(8,128)} %get-tuple-element.21, ...), kind=kLoop, calls=%fused_computation.15 | loop fusion | flops 4325376 | bytes 9469952 | tf_op jit(solution)/shard_map/add | solution.py:77
  652.4 3.9 copy.273
  (16 shorter events, 0.1 us)
Async XLA Ops:
  6.5 302.4 %all-reduce.7.cloned.1.call-start = ((), (), s32[]{:S(2)}) async-start(), calls=%async_computation.1 | async-start | bytes 16777216 | tf_op jit(solution)/shard_map/psum | solution.py:11
  17.1 2.8 copy-start.3
  17.1 611.4 %all-reduce.5.cloned.1.call-start = ((), (), s32[]{:S(2)}) async-start(), calls=%async_computation | async-start | bytes 16777216 | tf_op jit(solution)/shard_map/psum | solution.py:11
  18.2 8.9 %copy-start.9 = (s32[2]{0:T(128)S(1)}, s32[2]{0:T(128)}, u32[]{:S(2)}) copy-start(s32[2]{0:T(128)} %param.17) | copy-start | bytes 28
  18.2 9.6 %copy-start.7 = (s32[4,128]{1,0:T(4,128)S(1)}, s32[4,128]{1,0:T(4,128)}, u32[]{:S(2)}) copy-start(s32[4,128]{1,0:T(4,128)} %param.14) | copy-start | bytes 6148
  18.2 9.6 %copy-start.8 = (s32[4,128]{1,0:T(4,128)S(1)}, s32[4,128]{1,0:T(4,128)}, u32[]{:S(2)}) copy-start(s32[4,128]{1,0:T(4,128)} %param.12) | copy-start | bytes 6148
  18.2 302.9 %collective-permute-start = (f32[48,128]{0,1:T(8,128)S(1)}, f32[48,128]{0,1:T(8,128)S(1)}, u32[]{:S(2)}, u32[]{:S(2)}) collective-permute-start(f32[48,128]{0,1:T(8,128)S(1)} %fusion.10), channel_id=1, source_target_pairs={{0,4},{4,0},{8,12},{12,8},{1,5},{5,1},{9,13},{13,9},{2,6},{6,2},{1... | collective-permute-start | bytes 73736 | tf_op jit(solution)/shard_map/ppermute | solution.py:17
  23.8 298.4 %collective-permute-start.1 = (f32[48,64,1]{0,1,2:T(8,128)S(1)}, f32[48,64,1]{0,1,2:T(8,128)S(1)}, u32[]{:S(2)}, u32[]{:S(2)}) collective-permute-start(f32[48,64,1]{0,1,2:T(8,128)S(1)} %copy.283), channel_id=1, source_target_pairs={{0,1},{1,2},{2,3},{3,0},{4,5},{5,6},{6,7},{7,4},{8,9},{9,10},{10,1... | collective-permute-start | bytes 36872 | tf_op jit(solution)/shard_map/ppermute | solution.py:27
  24.7 297.5 %collective-permute-start.2 = (f32[48,64,1]{0,1,2:T(8,128)S(1)}, f32[48,64,1]{0,1,2:T(8,128)S(1)}, u32[]{:S(2)}, u32[]{:S(2)}) collective-permute-start(f32[48,64,1]{0,1,2:T(8,128)S(1)} %copy.284), channel_id=1, source_target_pairs={{1,0},{2,1},{3,2},{0,3},{5,4},{6,5},{7,6},{4,7},{9,8},{10,9},{11,1... | collective-permute-start | bytes 36872 | tf_op jit(solution)/shard_map/ppermute | solution.py:29
  28.4 8.0 %copy-start.2 = (f32[48,64,128]{0,2,1:T(8,128)S(1)}, f32[48,64,128]{0,2,1:T(8,128)}, u32[]{:S(2)}) copy-start(f32[48,64,128]{0,2,1:T(8,128)} %copy.264) | copy-start | bytes 4718596
  308.9 12.0 %copy-start.6 = (f32[4,128]{1,0:T(4,128)S(1)}, f32[4,128]{1,0:T(4,128)}, u32[]{:S(2)}) copy-start(f32[4,128]{1,0:T(4,128)} %param.13) | copy-start | bytes 6148
  308.9 13.1 %copy-start.5 = (f32[4,128]{1,0:T(4,128)S(1)}, f32[4,128]{1,0:T(4,128)}, u32[]{:S(2)}) copy-start(f32[4,128]{1,0:T(4,128)} %param.15) | copy-start | bytes 6148
  308.9 13.3 %copy-start.4 = (f32[64,128]{1,0:T(8,128)S(1)}, f32[64,128]{1,0:T(8,128)}, u32[]{:S(2)}) copy-start(f32[64,128]{1,0:T(8,128)} %param.11) | copy-start | bytes 98308
  333.2 3.3 copy-start
  337.6 14.7 %collective-permute-start.4 = (f32[48,64,1]{1,0,2:T(8,128)S(1)}, f32[48,64,1]{1,0,2:T(8,128)S(1)}, u32[]{:S(2)}, u32[]{:S(2)}) collective-permute-start(f32[48,64,1]{1,0,2:T(8,128)S(1)} %copy.265), channel_id=1, source_target_pairs={{0,1},{1,2},{2,3},{3,0},{4,5},{5,6},{6,7},{7,4},{8,9},{9,10},{10,1... | collective-permute-start | bytes 36872 | tf_op jit(solution)/shard_map/ppermute | solution.py:27
  337.7 10.4 %copy-start.1 = (f32[48,64,128]{0,2,1:T(8,128)S(1)}, f32[48,64,128]{0,2,1:T(8,128)}, u32[]{:S(2)}) copy-start(f32[48,64,128]{0,2,1:T(8,128)} %copy-done) | copy-start | bytes 4718596
  337.7 14.7 %collective-permute-start.5 = (f32[48,64,1]{1,0,2:T(8,128)S(1)}, f32[48,64,1]{1,0,2:T(8,128)S(1)}, u32[]{:S(2)}, u32[]{:S(2)}) collective-permute-start(f32[48,64,1]{1,0,2:T(8,128)S(1)} %copy.269), channel_id=1, source_target_pairs={{1,0},{2,1},{3,2},{0,3},{5,4},{6,5},{7,6},{4,7},{9,8},{10,9},{11,1... | collective-permute-start | bytes 36872 | tf_op jit(solution)/shard_map/ppermute | solution.py:29
  352.3 288.5 %collective-permute-start.3 = (f32[48,128]{0,1:T(8,128)S(1)}, f32[48,128]{0,1:T(8,128)S(1)}, u32[]{:S(2)}, u32[]{:S(2)}) collective-permute-start(f32[48,128]{0,1:T(8,128)S(1)} %fusion.11), channel_id=1, source_target_pairs={{0,4},{4,0},{8,12},{12,8},{1,5},{5,1},{9,13},{13,9},{2,6},{6,2},{1... | collective-permute-start | bytes 73736 | tf_op jit(solution)/shard_map/ppermute | solution.py:17
Sparse Core Ops, SparseCore 0:
  17.2 291.6 all-reduce.6
  336.6 291.9 all-reduce.4
where the time goes:
time: 666 us; the launch traced here: 663 us
  waiting for transfers between devices  544 us (82%)
  local copies, waits for them, and re-layouts  51.9 us (8%)
  other arithmetic  47 us (7%)
  between operations  14.4 us (2%)
    psum x2, waiting for transfers between devices, broadcast(): return lax.psum(block, axis)  544 us
    select_n x3, other arithmetic, broadcast(): jnp.where(lax.axis_index(axis) == holder, block, jnp.zeros_like(block))  20.6 us
  transfers between devices with their start and end apart: 8, of which 2 were waited for; matrix products, arithmetic and copies ran while one was open for 9% of the time, Pallas kernels for 0%

commit v1 on v0

v1 whole, which is shorter than its diff:
```python
import functools

import jax
import jax.numpy as jnp
from jax import lax
from jax.experimental import pallas as pl
from jax.experimental.pallas import tpu as pltpu
from jax.sharding import PartitionSpec as P

STEPS = 2
MESH = pl.DeviceIdType.MESH


def kernel(
    blocks,
    columns,
    state_hbm,
    diff_ref,
    rim_index_ref,
    rim_weight_ref,
    side_index_ref,
    side_weight_ref,
    tile_ref,
    offset_ref,
    out_hbm,
    u0,
    u1,
    u2,
    idx_send,
    w_send,
    idx_recv,
    w_recv,
    row_weights,
    col_send,
    col_recv,
    halo,
    row_send,
    row_recv,
    outer,
    rim_out,
    rim_recv,
    side_rows,
    side_out,
    side_recv,
    load_sem,
    store_sem,
    param_send_sem,
    param_recv_sem,
    col_send_sem,
    col_recv_sem,
    row_send_sem,
    row_recv_sem,
    rim_send_sem,
    rim_recv_sem,
    side_send_sem,
    side_recv_sem,
):
    var_count, tile_rows, tile_cols = u0.shape
    groups = tile_rows // 8
    nests = blocks - 2
    me = lax.axis_index("nest")
    t = lax.axis_index("tx")
    right, left = lax.rem(t + 1, columns), lax.rem(t + columns - 1, columns)
    parity = lax.rem(me, 2)
    mate = me + 1 - 2 * parity
    is_parent = me < 2
    is_nest = me >= 2
    at_edge = jnp.logical_or(t == 0, t == columns - 1)

    load = pltpu.make_async_copy(state_hbm, u0, load_sem)
    load.start()

    barrier = pltpu.get_barrier_semaphore()
    pl.semaphore_signal(barrier, inc=1, device_id={"tx": left}, device_id_type=MESH)
    pl.semaphore_signal(barrier, inc=1, device_id={"tx": right}, device_id_type=MESH)
    pl.semaphore_signal(barrier, inc=1, device_id={"nest": mate}, device_id_type=MESH)

    @pl.when(is_nest)
    def _():
        for p in range(2):
            pl.semaphore_signal(barrier, inc=1, device_id={"nest": p}, device_id_type=MESH)
        pl.semaphore_wait(barrier, 5)

    @pl.when(is_parent)
    def _():
        for b in range(nests):
            pl.semaphore_signal(barrier, inc=1, device_id={"nest": 2 + b}, device_id_type=MESH)
        pl.semaphore_wait(barrier, 3 + nests)

    row_id = lax.broadcasted_iota(jnp.int32, (tile_rows, tile_cols), 0)
    lane = lax.broadcasted_iota(jnp.int32, (tile_rows, tile_cols), 1)
    lane8 = lax.broadcasted_iota(jnp.int32, (8, tile_cols), 1)
    half = tile_rows

    def param_copies(p, slot):
        return (
            pltpu.make_async_remote_copy(
                src_ref=idx_send,
                dst_ref=idx_recv.at[slot],
                send_sem=param_send_sem.at[0, p],
                recv_sem=param_recv_sem.at[0, slot],
                device_id={"nest": p},
                device_id_type=MESH,
            ),
            pltpu.make_async_remote_copy(
                src_ref=w_send.at[p],
                dst_ref=w_recv.at[slot],
                send_sem=param_send_sem.at[1, p],
                recv_sem=param_recv_sem.at[1, slot],
                device_id={"nest": p},
                device_id_type=MESH,
            ),
        )

    @pl.when(is_nest)
    def _():
        offset = offset_ref[me // 2]
        tile = tile_ref[0, 0]
        stay = (t == 0) == (parity == 0)
        index = side_index_ref[...]
        weight = side_weight_ref[...]
        turned_index = jnp.concatenate([index[:, half:], index[:, :half]], axis=1)
        turned_weight = jnp.concatenate([weight[:, half:], weight[:, :half]], axis=1)
        idx_send[0:4] = rim_index_ref[...] + offset
        idx_send[4:8] = jnp.where(stay, index, turned_index) + offset
        for p in range(2):
            keep = jnp.where(tile == p, 1.0, 0.0)
            w_send[p, 0:4] = rim_weight_ref[...] * keep
            w_send[p, 4:8] = jnp.where(stay, weight, turned_weight) * keep
        for p in range(2):
            for copy in param_copies(p, me - 2):
                copy.start()

    load.wait()

    def col_copies(step):
        return (
            pltpu.make_async_remote_copy(
                src_ref=col_send.at[step],
                dst_ref=col_recv.at[step, 0],
                send_sem=col_send_sem.at[step, 0],
                recv_sem=col_recv_sem.at[step, 0],
                device_id={"tx": right},
                device_id_type=MESH,
            ),
            pltpu.make_async_remote_copy(
                src_ref=col_send.at[step],
                dst_ref=col_recv.at[step, 1],
                send_sem=col_send_sem.at[step, 1],
                recv_sem=col_recv_sem.at[step, 1],
                device_id={"tx": left},
                device_id_type=MESH,
            ),
            pltpu.make_async_remote_copy(
                src_ref=row_send.at[step],
                dst_ref=row_recv.at[step],
                send_sem=row_send_sem.at[step],
                recv_sem=row_recv_sem.at[step],
                device_id={"nest": mate},
                device_id_type=MESH,
            ),
        )

    def take_edges(step, v, tile, packed):
        last, first = tile[tile_rows - 1 :], tile[:1]
        row_send[step, pl.ds(v, 1), :] = jnp.where(parity == 0, last, first)

        @pl.when(is_parent)
        def _():
            outer[pl.ds(v, 1), :] = jnp.where(parity == 0, first, last)

        return jnp.where(lane // 2 == v, pltpu.roll(tile, 2 * v + 1, 1), packed)

    zeros = jnp.zeros((tile_rows, tile_cols), jnp.float32)
    col_send[0] = lax.fori_loop(0, var_count, lambda v, packed: take_edges(0, v, u0[v], packed), zeros)
    for copy in col_copies(0):
        copy.start()

    def rim_copies(step, slot, p):
        return pltpu.make_async_remote_copy(
            src_ref=rim_out.at[step, slot],
            dst_ref=rim_recv.at[step, p],
            send_sem=rim_send_sem.at[step, slot],
            recv_sem=rim_recv_sem.at[step, p],
            device_id={"nest": 2 + slot},
            device_id_type=MESH,
        )

    def side_copies(step, slot, p):
        return pltpu.make_async_remote_copy(
            src_ref=side_out.at[step, slot],
            dst_ref=side_recv.at[step, p],
            send_sem=side_send_sem.at[step, slot],
            recv_sem=side_recv_sem.at[step, p],
            device_id={"nest": 2 + slot},
            device_id_type=MESH,
        )

    def gather(vector, index):
        return jnp.take_along_axis(vector, index, axis=1, mode="promise_in_bounds")

    def column_of(row):
        return jnp.broadcast_to(lax.rem(row, tile_cols), (8, tile_cols))

    def weights_of(index, weight):
        return jnp.where(row_id == index // tile_cols, weight, 0.0)

    def side_rows_of(pair):
        low = lane8[:4] < half
        index = jnp.where(low, idx_recv[2 * pair, 4:8], idx_recv[2 * pair + 1, 4:8])
        weight = jnp.where(low, w_recv[2 * pair, 4:8], w_recv[2 * pair + 1, 4:8])
        return index, weight

    def sets_of(pair, what):
        if what == 2:
            return side_rows_of(pair)
        return idx_recv[2 * pair + what, 0:4], w_recv[2 * pair + what, 0:4]

    def prepare():
        for slot in range(nests):
            for p in range(2):
                @pl.when(me == p)
                def _():
                    for copy in param_copies(p, slot):
                        copy.wait_recv()
        for pair in range(nests // 2):
            for what in range(3):
                index, weight = sets_of(pair, what)
                for k in range(4):
                    row_weights[pair, what, k] = weights_of(index[k : k + 1], weight[k : k + 1])

    def interpolate(step, source):
        for pair in range(nests // 2):

            def run(whats):
                columns_of = {
                    (what, k): column_of(sets_of(pair, what)[0][k : k + 1]) for what in whats for k in range(4)
                }

                def one(v, carry):
                    totals = {what: jnp.zeros((8, tile_cols), jnp.float32) for what in whats}
                    for g in range(groups):
                        cells = source[v, 8 * g : 8 * g + 8, :]
                        for what in whats:
                            for k in range(4):
                                totals[what] += (
                                    gather(cells, columns_of[what, k]) * row_weights[pair, what, k, 8 * g : 8 * g + 8]
                                )
                    for what in whats:
                        value = jnp.sum(totals[what], axis=0, keepdims=True)
                        if what == 2:
                            side_rows[pl.ds(2 * v, 1), :] = value
                            side_rows[pl.ds(2 * v + 1, 1), :] = value
                        else:
                            rim_out[step, 2 * pair + what, pl.ds(v, 1), :] = value
                    return carry

                lax.fori_loop(0, var_count, one, 0)

            @pl.when(at_edge)
            def _():
                run((0, 1, 2))
                turned = side_rows[...].T
                for what in range(2):
                    side_out[step, 2 * pair + what] = turned[what * half : (what + 1) * half]
                for what in range(2):
                    for p in range(2):
                        @pl.when(me == p)
                        def _():
                            side_copies(step, 2 * pair + what, p).start()

            @pl.when(jnp.logical_not(at_edge))
            def _():
                run((0, 1))

            for what in range(2):
                for p in range(2):
                    @pl.when(me == p)
                    def _():
                        rim_copies(step, 2 * pair + what, p).start()

    @pl.when(is_parent)
    def _():
        side_rows[...] = jnp.zeros_like(side_rows)
        prepare()
        interpolate(0, u0)

    diffusivity = diff_ref

    for step in range(STEPS):
        source, target = ((u0, u1), (u1, u2))[step]
        to_right, to_left, to_mate = col_copies(step)
        to_right.wait_recv()
        to_left.wait_recv()
        to_mate.wait_recv()
        halo[...] = jnp.where(lane % 2 == 0, col_recv[step, 0], col_recv[step, 1])

        @pl.when(is_nest)
        def _():
            for p in range(2):
                rim_copies(step, 0, p).wait_recv()
            outer[...] = rim_recv[step, 0] + rim_recv[step, 1]

            @pl.when(at_edge)
            def _():
                for p in range(2):
                    side_copies(step, 0, p).wait_recv()
                own = lane % 2 == jnp.where(t == 0, 0, 1)
                halo[...] = jnp.where(own, side_recv[step, 0] + side_recv[step, 1], halo[...])

        def one(v, packed):
            u = source[v]
            mate_row = row_recv[step, pl.ds(v, 1), :]
            outer_row = outer[pl.ds(v, 1), :]
            top = jnp.where(parity == 0, outer_row, mate_row)
            bottom = jnp.where(parity == 0, mate_row, outer_row)
            ghost = pltpu.roll(halo[...], tile_cols - 1 - 2 * v, 1)
            left_side = pltpu.roll(jnp.where(lane == tile_cols - 1, ghost, u), 1, 1)
            right_side = pltpu.roll(jnp.where(lane == 0, ghost, u), tile_cols - 1, 1)
            above = jnp.where(row_id == 0, top, pltpu.roll(u, 1, 0))
            below = jnp.where(row_id == tile_rows - 1, bottom, pltpu.roll(u, tile_rows - 1, 0))
            laplace = above + below + left_side + right_side - 4.0 * u
            new = u + diff_ref[...] * laplace
            target[v] = new
            if step + 1 < STEPS:
                return take_edges(step + 1, v, new, packed)
            return packed

        packed = lax.fori_loop(0, var_count, one, zeros)
        if step + 1 < STEPS:
            col_send[step + 1] = packed
            for copy in col_copies(step + 1):
                copy.start()

            @pl.when(is_parent)
            def _():
                interpolate(step + 1, target)

    store = pltpu.make_async_copy(u2, out_hbm, store_sem)
    store.start()

    for step in range(STEPS):
        for copy in col_copies(step):
            copy.wait_send()

    @pl.when(is_nest)
    def _():
        for p in range(2):
            for copy in param_copies(p, 0):
                copy.wait_send()

    @pl.when(is_parent)
    def _():
        for step in range(STEPS):
            for slot in range(nests):
                rim_copies(step, slot, 0).wait_send()

                @pl.when(at_edge)
                def _():
                    side_copies(step, slot, 0).wait_send()

    store.wait()


def per_device(mesh_shape, *arrays):
    model_state = arrays[0]
    var_count, tile_rows, tile_cols = model_state.shape
    blocks, columns = mesh_shape["nest"], mesh_shape["tx"]
    nests = blocks - 2
    f32 = jnp.float32
    tile = (tile_rows, tile_cols)
    rows = (var_count, tile_cols)
    vmem = pl.BlockSpec(memory_space=pltpu.VMEM)
    smem = pl.BlockSpec(memory_space=pltpu.SMEM)
    hbm = pl.BlockSpec(memory_space=pl.ANY)
    dma = pltpu.SemaphoreType.DMA
    return pl.pallas_call(
        functools.partial(kernel, blocks, columns),
        out_shape=jax.ShapeDtypeStruct(model_state.shape, f32),
        in_specs=[hbm, vmem, vmem, vmem, vmem, vmem, smem, smem],
        out_specs=hbm,
        scratch_shapes=[
            pltpu.VMEM(model_state.shape, f32),
            pltpu.VMEM(model_state.shape, f32),
            pltpu.VMEM(model_state.shape, f32),
            pltpu.VMEM((8, tile_cols), jnp.int32),
            pltpu.VMEM((2, 8, tile_cols), f32),
            pltpu.VMEM((nests, 8, tile_cols), jnp.int32),
            pltpu.VMEM((nests, 8, tile_cols), f32),
            pltpu.VMEM((nests // 2, 3, 4) + tile, f32),
            pltpu.VMEM((STEPS,) + tile, f32),
            pltpu.VMEM((STEPS, 2) + tile, f32),
            pltpu.VMEM(tile, f32),
            pltpu.VMEM((STEPS,) + rows, f32),
            pltpu.VMEM((STEPS,) + rows, f32),
            pltpu.VMEM(rows, f32),
            pltpu.VMEM((STEPS, nests) + rows, f32),
            pltpu.VMEM((STEPS, 2) + rows, f32),
            pltpu.VMEM((tile_cols, tile_cols), f32),
            pltpu.VMEM((STEPS, nests) + tile, f32),
            pltpu.VMEM((STEPS, 2) + tile, f32),
            dma,
            dma,
            dma((2, 2)),
            dma((2, nests)),
            dma((STEPS, 2)),
            dma((STEPS, 2)),
            dma((STEPS,)),
            dma((STEPS,)),
            dma((STEPS, nests)),
            dma((STEPS, 2)),
            dma((STEPS, nests)),
            dma((STEPS, 2)),
        ],
        compiler_params=pltpu.CompilerParams(
            collective_id=0, has_side_effects=True, vmem_limit_bytes=40 * 2**20
        ),
        cost_estimate=pl.CostEstimate(
            flops=20 * model_state.size, bytes_accessed=8 * model_state.size, transcendentals=0
        ),
    )(*arrays)


def solution(mesh):
    placed = (
        P("parts", "nest", "tx"),
        P(("parts", "nest"), "tx"),
        P("nest", "tx"),
        P("nest", "tx"),
        P("nest", None),
        P("nest", None),
        P("nest", "tx"),
        P(),
    )
    return jax.shard_map(
        functools.partial(per_device, dict(mesh.shape)),
        mesh=mesh,
        in_specs=placed,
        out_specs=P("parts", "nest", "tx"),
        check_vma=False,
    )
```

time: 666 us -> 71.6 us (0.11)
  waiting for transfers between devices: 544 us -> 0 us
  Pallas kernels: 0 us -> 63.5 us
  other arithmetic: 47 us -> 0 us
  local copies, waits for them, and re-layouts: 51.9 us -> 6.68 us
  between operations: 14.4 us -> 0.67 us
    psum x2 -> x0, waiting for transfers between devices: 544 us -> none  [broadcast(): return lax.psum(block, axis)]
    pallas_call x0 -> x1, Pallas kernels: none -> 63.5 us  [per_device(): pl.pallas_call(functools.partial(kernel, blocks, columns), out_shape=jax....]
    select_n x13 -> x0, other arithmetic: 32.7 us -> none  [the longest x3 20.6 us: broadcast(): jnp.where(lax.axis_index(axis) == holder, block, jnp.zeros_like(block))]
    slice x8 -> x0, local copies, waits for them, and re-layouts: 27.7 us -> none  [the longest x1 8.49 us: per_device(): below_rows = jnp.concatenate([fields[:, 1:], bottom_ghost[:, None]], axis=1)]
    gather x4 -> x0, local copies, waits for them, and re-layouts: 12.9 us -> none  [interpolate(): picked = jnp.take(flat_tile, flat_index.reshape(-1), axis=1)]
    add x1 -> x0, other arithmetic: 10.7 us -> none  [per_device(): fields = fields + diffusivity[None] * laplace]
  transfers between devices with their start and end apart: 8 -> 0, of which waited for: 2 -> 0; matrix products, arithmetic and copies ran while one was open for 9% -> 0% of each run, Pallas kernels for 0% -> 0%
where the time goes in v1:
time: 71.6 us; the launch traced here: 70.9 us
  Pallas kernels  63.5 us (89%)
  local copies, waits for them, and re-layouts  6.68 us (9%)
    pallas_call x1, Pallas kernels, per_device(): pl.pallas_call(functools.partial(kernel, blocks, columns), out_shape=jax....  63.5 us
    unnamed x15, local copies, waits for them, and re-layouts  6.68 us

profile of v1, /device:TPU:16, one launch (start us, length us, event | category | flops | bytes accessed | tf_op | source)
XLA Modules:
  0.0 70.9 jit_solution(9320741365485886151)
XLA Ops:
  0.7 0.0 copy-start
  0.7 1.4 %copy-done = f32[48,64,128]{2,1,0:T(8,128)S(1)} copy-done((f32[48,64,128]{2,1,0:T(8,128)S(1)}, f32[48,64,128]{2,1,0:T(8,128)}, u32[]{:S(2)}) %copy-start) | copy-done | bytes 1572888
  2.1 0.0 copy-start.1
  2.1 0.8 %copy-done.1 = f32[64,128]{1,0:T(8,128)S(1)} copy-done((f32[64,128]{1,0:T(8,128)S(1)}, f32[64,128]{1,0:T(8,128)}, u32[]{:S(2)}) %copy-start.1) | copy-done | bytes 32792
  2.8 0.0 copy-start.2
  2.8 0.7 copy-done.2
  3.5 0.0 copy-start.3
  3.5 0.7 copy-done.3
  4.2 0.0 copy-start.4
  4.2 0.7 copy-done.4
  4.9 0.0 copy-start.5
  4.9 0.7 copy-done.5
  5.5 0.0 copy-start.6
  5.5 0.7 copy-done.6
  6.2 63.5 %shard_map.82 = f32[48,64,128]{2,1,0:T(8,128)S(1)} custom-call(f32[48,64,128]{2,1,0:T(8,128)S(1)} %copy-done, f32[64,128]{1,0:T(8,128)S(1)} %copy-done.1, s32[4,128]{1,0:T(4,128)S(1)} %copy-done.2, f32[4,128]{1,0:T(4,128)S(1)} %copy-done.3, s32[4,128]{1,0:T(4,128)S(1)} %copy-done.4, f32[4,128]{1,0:T(4,128)S(1)} %copy-done.5, s32[1,1]{1,0:T(1,128)S(6)} %copy.10.tile_ref, ...), custom_call_target="tpu_custom_call" | custom-call | flops 7864320 | bytes 3145728 | tf_op jit(solution)/shard_map/pallas_call | solution.py:377
  69.7 1.1 %copy.11 = f32[48,64,128]{2,1,0:T(8,128)} copy(f32[48,64,128]{2,1,0:T(8,128)S(1)} %shard_map.82) | data formatting | bytes 3145728
Async XLA Ops:
  0.7 1.4 %copy-start = (f32[48,64,128]{2,1,0:T(8,128)S(1)}, f32[48,64,128]{2,1,0:T(8,128)}, u32[]{:S(2)}) copy-start(f32[48,64,128]{2,1,0:T(8,128)} %state_hbm.1) | copy-start | bytes 4718596
  2.1 0.8 %copy-start.1 = (f32[64,128]{1,0:T(8,128)S(1)}, f32[64,128]{1,0:T(8,128)}, u32[]{:S(2)}) copy-start(f32[64,128]{1,0:T(8,128)} %diff_ref.1) | copy-start | bytes 98308
  2.8 0.7 copy-start.2
  3.5 0.7 copy-start.3
  4.2 0.7 copy-start.4
  4.9 0.7 copy-start.5
  5.5 0.7 copy-start.6

commit v2 on v1

--- a/solution.py
+++ b/solution.py
@@ -8,6 +8,9 @@
 from jax.sharding import PartitionSpec as P
 
 STEPS = 2
+CHUNK = 8
+BATCH = 4
+PICK = 16
 MESH = pl.DeviceIdType.MESH
 
 
@@ -15,22 +18,28 @@
     blocks,
     columns,
     state_hbm,
-    diff_ref,
-    rim_index_ref,
-    rim_weight_ref,
-    side_index_ref,
-    side_weight_ref,
+    diff_hbm,
+    rim_index_hbm,
+    rim_weight_hbm,
+    side_index_hbm,
+    side_weight_hbm,
     tile_ref,
     offset_ref,
     out_hbm,
     u0,
     u1,
     u2,
+    diff_ref,
+    rim_index_ref,
+    rim_weight_ref,
+    side_index_ref,
+    side_weight_ref,
     idx_send,
     w_send,
     idx_recv,
     w_recv,
     row_weights,
+    column_picks,
     col_send,
     col_recv,
     halo,
@@ -43,6 +52,7 @@
     side_out,
     side_recv,
     load_sem,
+    small_sem,
     store_sem,
     param_send_sem,
     param_recv_sem,
@@ -67,8 +77,28 @@
     is_nest = me >= 2
     at_edge = jnp.logical_or(t == 0, t == columns - 1)
 
-    load = pltpu.make_async_copy(state_hbm, u0, load_sem)
-    load.start()
+    smalls = [
+        pltpu.make_async_copy(source, target, small_sem.at[i])
+        for i, (source, target) in enumerate(
+            (
+                (rim_index_hbm, rim_index_ref),
+                (rim_weight_hbm, rim_weight_ref),
+                (side_index_hbm, side_index_ref),
+                (side_weight_hbm, side_weight_ref),
+                (diff_hbm, diff_ref),
+            )
+        )
+    ]
+    for copy in smalls:
+        copy.start()
+    loads = [
+        pltpu.make_async_copy(
+            state_hbm.at[pl.ds(i * CHUNK, CHUNK)], u0.at[pl.ds(i * CHUNK, CHUNK)], load_sem.at[i]
+        )
+        for i in range(var_count // CHUNK)
+    ]
+    for copy in loads:
+        copy.start()
 
     barrier = pltpu.get_barrier_semaphore()
     pl.semaphore_signal(barrier, inc=1, device_id={"tx": left}, device_id_type=MESH)
@@ -112,6 +142,9 @@
             ),
         )
 
+    for copy in smalls:
+        copy.wait()
+
     @pl.when(is_nest)
     def _():
         offset = offset_ref[me // 2]
@@ -130,8 +163,6 @@
         for p in range(2):
             for copy in param_copies(p, me - 2):
                 copy.start()
-
-    load.wait()
 
     def col_copies(step):
         return (
@@ -161,18 +192,23 @@
             ),
         )
 
-    def take_edges(step, v, tile, packed):
+    def take_edges(step, v, tile):
         last, first = tile[tile_rows - 1 :], tile[:1]
         row_send[step, pl.ds(v, 1), :] = jnp.where(parity == 0, last, first)
-
-        @pl.when(is_parent)
-        def _():
-            outer[pl.ds(v, 1), :] = jnp.where(parity == 0, first, last)
-
-        return jnp.where(lane // 2 == v, pltpu.roll(tile, 2 * v + 1, 1), packed)
-
-    zeros = jnp.zeros((tile_rows, tile_cols), jnp.float32)
-    col_send[0] = lax.fori_loop(0, var_count, lambda v, packed: take_edges(0, v, u0[v], packed), zeros)
+        outer[pl.ds(v, 1), :] = jnp.where(parity == 0, first, last)
+        col_send[step] = jnp.where(lane // 2 == v, pltpu.roll(tile, 2 * v + 1, 1), col_send[step])
+
+    col_send[...] = jnp.zeros_like(col_send)
+    for i, copy in enumerate(loads):
+        copy.wait()
+
+        def first_edges(trip, carry):
+            for j in range(BATCH):
+                v = i * CHUNK + trip * BATCH + j
+                take_edges(0, v, u0[v])
+            return carry
+
+        lax.fori_loop(0, CHUNK // BATCH, first_edges, 0)
     for copy in col_copies(0):
         copy.start()
 
@@ -196,11 +232,7 @@
             device_id_type=MESH,
         )
 
-    def gather(vector, index):
-        return jnp.take_along_axis(vector, index, axis=1, mode="promise_in_bounds")
-
-    def column_of(row):
-        return jnp.broadcast_to(lax.rem(row, tile_cols), (8, tile_cols))
+    square = lax.broadcasted_iota(jnp.int32, (tile_cols, tile_cols), 0)
 
     def weights_of(index, weight):
         return jnp.where(row_id == index // tile_cols, weight, 0.0)
@@ -228,41 +260,52 @@
                 index, weight = sets_of(pair, what)
                 for k in range(4):
                     row_weights[pair, what, k] = weights_of(index[k : k + 1], weight[k : k + 1])
+                    pick = jnp.where(square == lax.rem(index[k : k + 1], tile_cols), 1.0, 0.0).astype(jnp.bfloat16)
+                    for part in range(2):
+                        column_picks[
+                            pair, what, part * tile_cols : (part + 1) * tile_cols, k * tile_cols : (k + 1) * tile_cols
+                        ] = pick
 
     def interpolate(step, source):
         for pair in range(nests // 2):
 
             def run(whats):
-                columns_of = {
-                    (what, k): column_of(sets_of(pair, what)[0][k : k + 1]) for what in whats for k in range(4)
-                }
-
-                def one(v, carry):
-                    totals = {what: jnp.zeros((8, tile_cols), jnp.float32) for what in whats}
-                    for g in range(groups):
-                        cells = source[v, 8 * g : 8 * g + 8, :]
-                        for what in whats:
-                            for k in range(4):
-                                totals[what] += (
-                                    gather(cells, columns_of[what, k]) * row_weights[pair, what, k, 8 * g : 8 * g + 8]
-                                )
+                def one(trip, carry):
+                    these = pl.ds(trip * PICK, PICK)
+                    cells = source[these].reshape(PICK * tile_rows, tile_cols)
+                    high = cells.astype(jnp.bfloat16)
+                    low = (cells - high.astype(jnp.float32)).astype(jnp.bfloat16)
+                    parts = jnp.concatenate([high, low], axis=1)
                     for what in whats:
-                        value = jnp.sum(totals[what], axis=0, keepdims=True)
+                        total = jnp.zeros((PICK, 8, tile_cols), jnp.float32)
+                        for two in range(2):
+                            span = slice(2 * two * tile_cols, 2 * (two + 1) * tile_cols)
+                            picked = jnp.dot(
+                                parts, column_picks[pair, what, :, span], preferred_element_type=jnp.float32
+                            )
+                            for k in range(2):
+                                one_k = picked[:, k * tile_cols : (k + 1) * tile_cols]
+                                weighted = one_k.reshape(PICK, groups, 8, tile_cols) * row_weights[
+                                    pair, what, 2 * two + k
+                                ].reshape(1, groups, 8, tile_cols)
+                                total = total + jnp.sum(weighted, axis=1)
+                        value = jnp.sum(total, axis=1)
                         if what == 2:
-                            side_rows[pl.ds(2 * v, 1), :] = value
-                            side_rows[pl.ds(2 * v + 1, 1), :] = value
+                            side_rows[these, :] = value
                         else:
-                            rim_out[step, 2 * pair + what, pl.ds(v, 1), :] = value
+                            rim_out[step, 2 * pair + what, these, :] = value
                     return carry
 
-                lax.fori_loop(0, var_count, one, 0)
+                lax.fori_loop(0, var_count // PICK, one, 0)
 
             @pl.when(at_edge)
             def _():
                 run((0, 1, 2))
                 turned = side_rows[...].T
                 for what in range(2):
-                    side_out[step, 2 * pair + what] = turned[what * half : (what + 1) * half]
+                    side_out[step, 2 * pair + what] = jnp.take_along_axis(
+                        turned[what * half : (what + 1) * half], lane // 2, axis=1, mode="promise_in_bounds"
+                    )
                 for what in range(2):
                     for p in range(2):
                         @pl.when(me == p)
@@ -285,7 +328,9 @@
         prepare()
         interpolate(0, u0)
 
-    diffusivity = diff_ref
+    def store(chunk):
+        these = pl.ds(chunk * CHUNK, CHUNK)
+        return pltpu.make_async_copy(u2.at[these], out_hbm.at[these], store_sem.at[chunk])
 
     for step in range(STEPS):
         source, target = ((u0, u1), (u1, u2))[step]
@@ -308,7 +353,7 @@
                 own = lane % 2 == jnp.where(t == 0, 0, 1)
                 halo[...] = jnp.where(own, side_recv[step, 0] + side_recv[step, 1], halo[...])
 
-        def one(v, packed):
+        def update(v):
             u = source[v]
             mate_row = row_recv[step, pl.ds(v, 1), :]
             outer_row = outer[pl.ds(v, 1), :]
@@ -323,12 +368,21 @@
             new = u + diff_ref[...] * laplace
             target[v] = new
             if step + 1 < STEPS:
-                return take_edges(step + 1, v, new, packed)
-            return packed
-
-        packed = lax.fori_loop(0, var_count, one, zeros)
+                take_edges(step + 1, v, new)
+
+        def one(chunk, carry):
+            def inner(trip, carry):
+                for j in range(BATCH):
+                    update(chunk * CHUNK + trip * BATCH + j)
+                return carry
+
+            lax.fori_loop(0, CHUNK // BATCH, inner, 0)
+            if step == STEPS - 1:
+                store(chunk).start()
+            return carry
+
+        lax.fori_loop(0, var_count // CHUNK, one, 0)
         if step + 1 < STEPS:
-            col_send[step + 1] = packed
             for copy in col_copies(step + 1):
                 copy.start()
 
@@ -336,9 +390,6 @@
             def _():
                 interpolate(step + 1, target)
 
-    store = pltpu.make_async_copy(u2, out_hbm, store_sem)
-    store.start()
-
     for step in range(STEPS):
         for copy in col_copies(step):
             copy.wait_send()
@@ -359,7 +410,8 @@
                 def _():
                     side_copies(step, slot, 0).wait_send()
 
-    store.wait()
+    for chunk in range(var_count // CHUNK):
+        store(chunk).wait()
 
 
 def per_device(mesh_shape, *arrays):
@@ -370,24 +422,29 @@
     f32 = jnp.float32
     tile = (tile_rows, tile_cols)
     rows = (var_count, tile_cols)
-    vmem = pl.BlockSpec(memory_space=pltpu.VMEM)
     smem = pl.BlockSpec(memory_space=pltpu.SMEM)
-    hbm = pl.BlockSpec(memory_space=pl.ANY)
+    hbm = pl.BlockSpec(memory_space=pltpu.HBM)
     dma = pltpu.SemaphoreType.DMA
     return pl.pallas_call(
         functools.partial(kernel, blocks, columns),
         out_shape=jax.ShapeDtypeStruct(model_state.shape, f32),
-        in_specs=[hbm, vmem, vmem, vmem, vmem, vmem, smem, smem],
+        in_specs=[hbm] * 6 + [smem] * 2,
         out_specs=hbm,
         scratch_shapes=[
             pltpu.VMEM(model_state.shape, f32),
             pltpu.VMEM(model_state.shape, f32),
             pltpu.VMEM(model_state.shape, f32),
+            pltpu.VMEM(tile, f32),
+            pltpu.VMEM((4, tile_cols), jnp.int32),
+            pltpu.VMEM((4, tile_cols), f32),
+            pltpu.VMEM((4, tile_cols), jnp.int32),
+            pltpu.VMEM((4, tile_cols), f32),
             pltpu.VMEM((8, tile_cols), jnp.int32),
             pltpu.VMEM((2, 8, tile_cols), f32),
             pltpu.VMEM((nests, 8, tile_cols), jnp.int32),
             pltpu.VMEM((nests, 8, tile_cols), f32),
             pltpu.VMEM((nests // 2, 3, 4) + tile, f32),
+            pltpu.VMEM((nests // 2, 3, 2 * tile_cols, 4 * tile_cols), jnp.bfloat16),
             pltpu.VMEM((STEPS,) + tile, f32),
             pltpu.VMEM((STEPS, 2) + tile, f32),
             pltpu.VMEM(tile, f32),
@@ -399,8 +456,9 @@
             pltpu.VMEM((tile_cols, tile_cols), f32),
             pltpu.VMEM((STEPS, nests) + tile, f32),
             pltpu.VMEM((STEPS, 2) + tile, f32),
-            dma,
-            dma,
+            dma((var_count // CHUNK,)),
+            dma((5,)),
+            dma((var_count // CHUNK,)),
             dma((2, 2)),
             dma((2, nests)),
             dma((STEPS, 2)),
@@ -413,7 +471,7 @@
             dma((STEPS, 2)),
         ],
         compiler_params=pltpu.CompilerParams(
-            collective_id=0, has_side_effects=True, vmem_limit_bytes=40 * 2**20
+            collective_id=0, has_side_effects=True, vmem_limit_bytes=64 * 2**20
         ),
         cost_estimate=pl.CostEstimate(
             flops=20 * model_state.size, bytes_accessed=8 * model_state.size, transcendentals=0

time: 71.6 us -> 27.9 us (0.39)
  Pallas kernels: 63.5 us -> 24.4 us
  local copies, waits for them, and re-layouts: 6.68 us -> 2.73 us
    pallas_call x1, Pallas kernels: 63.5 us -> 24.4 us  [per_device(): pl.pallas_call(functools.partial(kernel, blocks, columns), out_shape=jax....]
    unnamed x15 -> x1, local copies, waits for them, and re-layouts: 6.68 us -> 2.73 us
where the time goes in v2:
time: 27.9 us; the launch traced here: 27.7 us
  Pallas kernels  24.4 us (87%)
  local copies, waits for them, and re-layouts  2.73 us (10%)
  between operations  0.66 us (2%)
    pallas_call x1, Pallas kernels, per_device(): pl.pallas_call(functools.partial(kernel, blocks, columns), out_shape=jax....  24.4 us
    unnamed x1, local copies, waits for them, and re-layouts  2.73 us

profile of v2, /device:TPU:16, one launch (start us, length us, event | category | flops | bytes accessed | tf_op | source)
XLA Modules:
  0.0 27.7 jit_solution(4701650000876051433)
XLA Ops:
  0.7 24.4 %shard_map.82 = f32[48,64,128]{2,1,0:T(8,128)} custom-call(f32[48,64,128]{2,1,0:T(8,128)} %state_hbm.1, f32[64,128]{1,0:T(8,128)} %diff_hbm.1, s32[4,128]{1,0:T(4,128)} %rim_index_hbm.1, f32[4,128]{1,0:T(4,128)} %rim_weight_hbm.1, s32[4,128]{1,0:T(4,128)} %side_index_hbm.1, f32[4,128]{1,0:T(4,128)} %side_weight_hbm.1, s32[1,1]{1,0:T(1,128)S(6)} %copy.10.tile_ref, ...), custom_call_target="tpu_custom_call" | custom-call | flops 7864320 | bytes 3145728 | tf_op jit(solution)/shard_map/pallas_call | solution.py:428
  25.0 2.7 %copy.11 = f32[48,64,128]{2,1,0:T(8,128)} copy(f32[48,64,128]{2,1,0:T(8,128)} %shard_map.82) | data formatting | bytes 3145728

commit v3 on v2

--- a/solution.py
+++ b/solution.py
@@ -9,7 +9,7 @@
 
 STEPS = 2
 CHUNK = 8
-BATCH = 4
+BATCH = 8
 PICK = 16
 MESH = pl.DeviceIdType.MESH
 
@@ -40,6 +40,7 @@
     w_recv,
     row_weights,
     column_picks,
+    beside,
     col_send,
     col_recv,
     halo,
@@ -232,6 +233,11 @@
             device_id_type=MESH,
         )
 
+    def split(cells):
+        high = cells.astype(jnp.bfloat16)
+        low = (cells - high.astype(jnp.float32)).astype(jnp.bfloat16)
+        return jnp.concatenate([high, low], axis=1)
+
     square = lax.broadcasted_iota(jnp.int32, (tile_cols, tile_cols), 0)
 
     def weights_of(index, weight):
@@ -272,10 +278,7 @@
             def run(whats):
                 def one(trip, carry):
                     these = pl.ds(trip * PICK, PICK)
-                    cells = source[these].reshape(PICK * tile_rows, tile_cols)
-                    high = cells.astype(jnp.bfloat16)
-                    low = (cells - high.astype(jnp.float32)).astype(jnp.bfloat16)
-                    parts = jnp.concatenate([high, low], axis=1)
+                    parts = split(source[these].reshape(PICK * tile_rows, tile_cols))
                     for what in whats:
                         total = jnp.zeros((PICK, 8, tile_cols), jnp.float32)
                         for two in range(2):
@@ -322,6 +325,11 @@
                     def _():
                         rim_copies(step, 2 * pair + what, p).start()
 
+    distance = square - lax.broadcasted_iota(jnp.int32, (tile_cols, tile_cols), 1)
+    neighbours = jnp.where((distance == 1) | (distance == -1), 1.0, 0.0).astype(jnp.bfloat16)
+    for part in range(2):
+        beside[part * tile_cols : (part + 1) * tile_cols] = neighbours
+
     @pl.when(is_parent)
     def _():
         side_rows[...] = jnp.zeros_like(side_rows)
@@ -329,7 +337,7 @@
         interpolate(0, u0)
 
     def store(chunk):
-        these = pl.ds(chunk * CHUNK, CHUNK)
+        these = pl.ds(chunk * BATCH, BATCH)
         return pltpu.make_async_copy(u2.at[these], out_hbm.at[these], store_sem.at[chunk])
 
     for step in range(STEPS):
@@ -338,7 +346,11 @@
         to_right.wait_recv()
         to_left.wait_recv()
         to_mate.wait_recv()
-        halo[...] = jnp.where(lane % 2 == 0, col_recv[step, 0], col_recv[step, 1])
+        halo[...] = jnp.where(
+            lane % 2 == 0,
+            pltpu.roll(col_recv[step, 1], tile_cols - 1, 1),
+            pltpu.roll(col_recv[step, 0], 1, 1),
+        )
 
         @pl.when(is_nest)
         def _():
@@ -350,38 +362,36 @@
             def _():
                 for p in range(2):
                     side_copies(step, 0, p).wait_recv()
-                own = lane % 2 == jnp.where(t == 0, 0, 1)
+                own = lane % 2 == jnp.where(t == 0, 1, 0)
                 halo[...] = jnp.where(own, side_recv[step, 0] + side_recv[step, 1], halo[...])
 
-        def update(v):
-            u = source[v]
+        def update(v, u, sides):
             mate_row = row_recv[step, pl.ds(v, 1), :]
             outer_row = outer[pl.ds(v, 1), :]
             top = jnp.where(parity == 0, outer_row, mate_row)
             bottom = jnp.where(parity == 0, mate_row, outer_row)
             ghost = pltpu.roll(halo[...], tile_cols - 1 - 2 * v, 1)
-            left_side = pltpu.roll(jnp.where(lane == tile_cols - 1, ghost, u), 1, 1)
-            right_side = pltpu.roll(jnp.where(lane == 0, ghost, u), tile_cols - 1, 1)
+            sides = sides + jnp.where((lane == 0) | (lane == tile_cols - 1), ghost, 0.0)
             above = jnp.where(row_id == 0, top, pltpu.roll(u, 1, 0))
             below = jnp.where(row_id == tile_rows - 1, bottom, pltpu.roll(u, tile_rows - 1, 0))
-            laplace = above + below + left_side + right_side - 4.0 * u
+            laplace = above + below + sides - 4.0 * u
             new = u + diff_ref[...] * laplace
             target[v] = new
             if step + 1 < STEPS:
                 take_edges(step + 1, v, new)
 
         def one(chunk, carry):
-            def inner(trip, carry):
-                for j in range(BATCH):
-                    update(chunk * CHUNK + trip * BATCH + j)
-                return carry
-
-            lax.fori_loop(0, CHUNK // BATCH, inner, 0)
+            cells = source[pl.ds(chunk * BATCH, BATCH)]
+            sides = jnp.dot(
+                split(cells.reshape(BATCH * tile_rows, tile_cols)), beside[...], preferred_element_type=jnp.float32
+            )
+            for j in range(BATCH):
+                update(chunk * BATCH + j, cells[j], sides[j * tile_rows : (j + 1) * tile_rows])
             if step == STEPS - 1:
                 store(chunk).start()
             return carry
 
-        lax.fori_loop(0, var_count // CHUNK, one, 0)
+        lax.fori_loop(0, var_count // BATCH, one, 0)
         if step + 1 < STEPS:
             for copy in col_copies(step + 1):
                 copy.start()
@@ -410,7 +420,7 @@
                 def _():
                     side_copies(step, slot, 0).wait_send()
 
-    for chunk in range(var_count // CHUNK):
+    for chunk in range(var_count // BATCH):
         store(chunk).wait()
 
 
@@ -445,6 +455,7 @@
             pltpu.VMEM((nests, 8, tile_cols), f32),
             pltpu.VMEM((nests // 2, 3, 4) + tile, f32),
             pltpu.VMEM((nests // 2, 3, 2 * tile_cols, 4 * tile_cols), jnp.bfloat16),
+            pltpu.VMEM((2 * tile_cols, tile_cols), jnp.bfloat16),
             pltpu.VMEM((STEPS,) + tile, f32),
             pltpu.VMEM((STEPS, 2) + tile, f32),
             pltpu.VMEM(tile, f32),
@@ -458,7 +469,7 @@
             pltpu.VMEM((STEPS, 2) + tile, f32),
             dma((var_count // CHUNK,)),
             dma((5,)),
-            dma((var_count // CHUNK,)),
+            dma((var_count // BATCH,)),
             dma((2, 2)),
             dma((2, nests)),
             dma((STEPS, 2)),

time: 27.9 us -> 25.7 us (0.921)
  Pallas kernels: 24.4 us -> 22.1 us
    pallas_call x1, Pallas kernels: 24.4 us -> 22.1 us  [per_device(): pl.pallas_call(functools.partial(kernel, blocks, columns), out_shape=jax....]
where the time goes in v3:
time: 25.7 us; the launch traced here: 25.5 us
  Pallas kernels  22.1 us (86%)
  local copies, waits for them, and re-layouts  2.73 us (11%)
  between operations  0.66 us (3%)
    pallas_call x1, Pallas kernels, per_device(): pl.pallas_call(functools.partial(kernel, blocks, columns), out_shape=jax....  22.1 us
    unnamed x1, local copies, waits for them, and re-layouts  2.73 us

profile of v3, /device:TPU:16, one launch (start us, length us, event | category | flops | bytes accessed | tf_op | source)
XLA Modules:
  0.0 25.5 jit_solution(14875132662797143972)
XLA Ops:
  0.7 22.1 %shard_map.82 = f32[48,64,128]{2,1,0:T(8,128)} custom-call(f32[48,64,128]{2,1,0:T(8,128)} %state_hbm.1, f32[64,128]{1,0:T(8,128)} %diff_hbm.1, s32[4,128]{1,0:T(4,128)} %rim_index_hbm.1, f32[4,128]{1,0:T(4,128)} %rim_weight_hbm.1, s32[4,128]{1,0:T(4,128)} %side_index_hbm.1, f32[4,128]{1,0:T(4,128)} %side_weight_hbm.1, s32[1,1]{1,0:T(1,128)S(6)} %copy.10.tile_ref, ...), custom_call_target="tpu_custom_call" | custom-call | flops 7864320 | bytes 3145728 | tf_op jit(solution)/shard_map/pallas_call | solution.py:438
  22.8 2.7 %copy.11 = f32[48,64,128]{2,1,0:T(8,128)} copy(f32[48,64,128]{2,1,0:T(8,128)} %shard_map.82) | data formatting | bytes 3145728

commit v4 on v3

--- a/solution.py
+++ b/solution.py
@@ -352,18 +352,28 @@
             pltpu.roll(col_recv[step, 0], 1, 1),
         )
 
-        @pl.when(is_nest)
-        def _():
-            for p in range(2):
-                rim_copies(step, 0, p).wait_recv()
-            outer[...] = rim_recv[step, 0] + rim_recv[step, 1]
-
-            @pl.when(at_edge)
+        own = lane % 2 == jnp.where(t == 0, 1, 0)
+        if step < STEPS - 1:
+
+            @pl.when(is_nest)
             def _():
                 for p in range(2):
-                    side_copies(step, 0, p).wait_recv()
-                own = lane % 2 == jnp.where(t == 0, 1, 0)
-                halo[...] = jnp.where(own, side_recv[step, 0] + side_recv[step, 1], halo[...])
+                    rim_copies(step, 0, p).wait_recv()
+                outer[...] = rim_recv[step, 0] + rim_recv[step, 1]
+
+                @pl.when(at_edge)
+                def _():
+                    for p in range(2):
+                        side_copies(step, 0, p).wait_recv()
+                    halo[...] = jnp.where(own, side_recv[step, 0] + side_recv[step, 1], halo[...])
+        else:
+            @pl.when(is_nest)
+            def _():
+                outer[...] = jnp.zeros_like(outer)
+
+                @pl.when(at_edge)
+                def _():
+                    halo[...] = jnp.where(own, 0.0, halo[...])
 
         def update(v, u, sides):
             mate_row = row_recv[step, pl.ds(v, 1), :]
@@ -388,7 +398,10 @@
             for j in range(BATCH):
                 update(chunk * BATCH + j, cells[j], sides[j * tile_rows : (j + 1) * tile_rows])
             if step == STEPS - 1:
-                store(chunk).start()
+
+                @pl.when(is_parent)
+                def _():
+                    store(chunk).start()
             return carry
 
         lax.fori_loop(0, var_count // BATCH, one, 0)
@@ -399,6 +412,55 @@
             @pl.when(is_parent)
             def _():
                 interpolate(step + 1, target)
+
+    @pl.when(is_nest)
+    def _():
+        last = STEPS - 1
+        for p in range(2):
+            rim_copies(last, 0, p).wait_recv()
+        outer[...] = rim_recv[last, 0] + rim_recv[last, 1]
+
+        def add_rims(chunk, row):
+            for j in range(BATCH):
+                v = chunk * BATCH + j
+                u2[v, row : row + 1, :] = u2[v, row : row + 1, :] + diff_ref[row : row + 1] * outer[pl.ds(v, 1), :]
+
+        def add_to_row(chunk):
+            @pl.when(parity == 0)
+            def _():
+                add_rims(chunk, 0)
+
+            @pl.when(parity == 1)
+            def _():
+                add_rims(chunk, tile_rows - 1)
+
+        @pl.when(at_edge)
+        def _():
+            for p in range(2):
+                side_copies(last, 0, p).wait_recv()
+            own = lane % 2 == jnp.where(t == 0, 1, 0)
+            halo[...] = jnp.where(own, side_recv[last, 0] + side_recv[last, 1], 0.0)
+
+            def finish(chunk, carry):
+                add_to_row(chunk)
+                for j in range(BATCH):
+                    v = chunk * BATCH + j
+                    ghost = pltpu.roll(halo[...], tile_cols - 1 - 2 * v, 1)
+                    ghost = jnp.where((lane == 0) | (lane == tile_cols - 1), ghost, 0.0)
+                    u2[v] = u2[v] + diff_ref[...] * ghost
+                store(chunk).start()
+                return carry
+
+            lax.fori_loop(0, var_count // BATCH, finish, 0)
+
+        @pl.when(jnp.logical_not(at_edge))
+        def _():
+            def finish(chunk, carry):
+                add_to_row(chunk)
+                store(chunk).start()
+                return carry
+
+            lax.fori_loop(0, var_count // BATCH, finish, 0)
 
     for step in range(STEPS):
         for copy in col_copies(step):

time: 25.7 us -> 26.6 us (1.035)
  Pallas kernels: 22.1 us -> 23 us
    pallas_call x1, Pallas kernels: 22.1 us -> 23 us  [per_device(): pl.pallas_call(functools.partial(kernel, blocks, columns), out_shape=jax....]
where the time goes in v4:
time: 26.6 us; the launch traced here: 26.4 us
  Pallas kernels  23 us (86%)
  local copies, waits for them, and re-layouts  2.73 us (10%)
  between operations  0.66 us (2%)
    pallas_call x1, Pallas kernels, per_device(): pl.pallas_call(functools.partial(kernel, blocks, columns), out_shape=jax....  23 us
    unnamed x1, local copies, waits for them, and re-layouts  2.73 us

profile of v4, /device:TPU:16, one launch (start us, length us, event | category | flops | bytes accessed | tf_op | source)
XLA Modules:
  0.0 26.4 jit_solution(10816623337377673657)
XLA Ops:
  0.7 23.0 %shard_map.82 = f32[48,64,128]{2,1,0:T(8,128)} custom-call(f32[48,64,128]{2,1,0:T(8,128)} %state_hbm.1, f32[64,128]{1,0:T(8,128)} %diff_hbm.1, s32[4,128]{1,0:T(4,128)} %rim_index_hbm.1, f32[4,128]{1,0:T(4,128)} %rim_weight_hbm.1, s32[4,128]{1,0:T(4,128)} %side_index_hbm.1, f32[4,128]{1,0:T(4,128)} %side_weight_hbm.1, s32[1,1]{1,0:T(1,128)S(6)} %copy.10.tile_ref, ...), custom_call_target="tpu_custom_call" | custom-call | flops 7864320 | bytes 3145728 | tf_op jit(solution)/shard_map/pallas_call | solution.py:500
  23.7 2.7 %copy.11 = f32[48,64,128]{2,1,0:T(8,128)} copy(f32[48,64,128]{2,1,0:T(8,128)} %shard_map.82) | data formatting | bytes 3145728

commit v5 on v3

--- a/solution.py
+++ b/solution.py
@@ -10,7 +10,7 @@
 STEPS = 2
 CHUNK = 8
 BATCH = 8
-PICK = 16
+PICK = 24
 MESH = pl.DeviceIdType.MESH
 
 

time: 25.7 us -> 25.5 us (level)
  no operation moved by 1% of the time
where the time goes in v5:
time: 25.5 us; the launch traced here: 25.4 us
  Pallas kernels  22 us (86%)
  local copies, waits for them, and re-layouts  2.73 us (11%)
  between operations  0.66 us (3%)
    pallas_call x1, Pallas kernels, per_device(): pl.pallas_call(functools.partial(kernel, blocks, columns), out_shape=jax....  22 us
    unnamed x1, local copies, waits for them, and re-layouts  2.73 us

profile of v5, /device:TPU:16, one launch (start us, length us, event | category | flops | bytes accessed | tf_op | source)
XLA Modules:
  0.0 25.4 jit_solution(1158026711375888281)
XLA Ops:
  0.7 22.0 %shard_map.82 = f32[48,64,128]{2,1,0:T(8,128)} custom-call(f32[48,64,128]{2,1,0:T(8,128)} %state_hbm.1, f32[64,128]{1,0:T(8,128)} %diff_hbm.1, s32[4,128]{1,0:T(4,128)} %rim_index_hbm.1, f32[4,128]{1,0:T(4,128)} %rim_weight_hbm.1, s32[4,128]{1,0:T(4,128)} %side_index_hbm.1, f32[4,128]{1,0:T(4,128)} %side_weight_hbm.1, s32[1,1]{1,0:T(1,128)S(6)} %copy.10.tile_ref, ...), custom_call_target="tpu_custom_call" | custom-call | flops 7864320 | bytes 3145728 | tf_op jit(solution)/shard_map/pallas_call | solution.py:438
  22.6 2.7 %copy.11 = f32[48,64,128]{2,1,0:T(8,128)} copy(f32[48,64,128]{2,1,0:T(8,128)} %shard_map.82) | data formatting | bytes 3145728
